TPU v7x, 32 devices: a whole 2x2x4 slice. The times are simulated.
32 devices in a mesh: fsdp: 2 (over x), heads: 4 (over z), tensor: 4 (over y, core).
Axes of the slice: x: 2, y: 2, z: 4, core: 2. Of those that a mesh axis runs over, the one named last changes fastest.
Arguments:
- tokens: bfloat16 [8, 256, 768], P(('fsdp', 'tensor')), may hold values from -6 to 6
- valid_mask: int32 [8, 256], P(('fsdp', 'tensor')), may hold values from 0 to 1, as said below
- routes: int32 [8, 256, 2], P('fsdp'), may hold values from 0 to 31, all different within a row; in each aligned block of 1024 rows (0 to 1023, 1024 to 2047, ..., all dimensions but the last counted through in order) at most 128 rows name the same one
- teacher: bfloat16 [8, 256, 768], P(('fsdp', 'tensor')), may hold values from -6 to 6
- gain_one: bfloat16 [768], P(('fsdp', 'tensor')), may hold values from 0.099609375 to 1.8984375
- qkv_weight: bfloat16 [768, 12, 192], P(('fsdp', 'tensor'), 'heads'), may hold values from -0.3125 to 0.3125
- out_weight: bfloat16 [12, 64, 768], P('heads', None, ('fsdp', 'tensor')), may hold values from -1 to 1
- gain_two: bfloat16 [768], P(('fsdp', 'tensor')), may hold values from 0.099609375 to 1.8984375
- router_weight: bfloat16 [768, 32], P(('fsdp', 'tensor')), may hold values from -0.109375 to 0.109375
- expert_up: bfloat16 [32, 768, 3072], P('heads', 'fsdp', 'tensor'), may hold values from -0.21875 to 0.21875
- expert_down: bfloat16 [32, 3072, 768], P('heads', 'tensor', 'fsdp'), may hold values from -3.5 to 3.5
Outputs:
- result: bfloat16 [8, 256, 768], P(('fsdp', 'tensor'))
- loss_terms: float32 [8], P(('fsdp', 'tensor'))
- tokens_grad: float32 [8, 256, 768], P(('fsdp', 'tensor'))
- gain_one_grad: float32 [768], P(('fsdp', 'tensor'))
- qkv_grad: float32 [768, 12, 192], P(('fsdp', 'tensor'), 'heads')
- out_weight_grad: float32 [12, 64, 768], P('heads', None, ('fsdp', 'tensor'))
- gain_two_grad: float32 [768], P(('fsdp', 'tensor'))
- router_grad: float32 [768, 32], P(('fsdp', 'tensor'))
- expert_up_grad: float32 [32, 768, 3072], P('heads', 'fsdp', 'tensor')
- expert_down_grad: float32 [32, 3072, 768], P('heads', 'tensor', 'fsdp')
Inputs may be any that keep to these rules, and one draw needn't show every extreme that they name: `valid_mask`: an image's valid tokens are its first ones, 1 to 197 of them; some image has exactly 197. `routes`: each row names 2 different experts. In the 1024 rows of each index of fsdp no expert is named more than 128 times, a bound that some block reaches.
All inputs are finite; a program needn't handle non-finite values.
Results may differ from a plain program's by a relative error of at most 0.012.
The roundings to bfloat16 on the way count: a program that leaves them out, or rounds other values in their place, can miss the bound.
Values may be sent and summed in bfloat16 or wider, within the bound.
A program may use at most 192 MiB of HBM per device.

v0:
```python
import jax
import jax.numpy as jnp
from jax import lax
from jax.sharding import PartitionSpec as P

EPSILON = 1e-06
MASKED = -1e30
ROOT_HALF = 0.7071067811865476
DENSITY = 0.3989422804014327


def normalize(values):
    center = values - jnp.mean(values, -1, keepdims=True)
    inv_std = lax.rsqrt(jnp.mean(center * center, -1, keepdims=True) + EPSILON)
    return (center * inv_std, inv_std)


def norm_back(gradient, normed, inv_std, gain_vector):
    weighted = gradient * gain_vector
    gain_grad = jnp.sum(gradient * normed, axis=(0, 1))
    inner = (
        weighted
        - jnp.mean(weighted, -1, keepdims=True)
        - normed * jnp.mean(weighted * normed, -1, keepdims=True)
    )
    return (inner * inv_std, gain_grad)


def scores_of(queries, key_rows, keys_ok, score_scale):
    raw_scores = (
        jnp.einsum("iqhe,ikhe->ihqk", queries, key_rows, preferred_element_type=jnp.float32)
        * score_scale
    )
    return jnp.where(keys_ok, raw_scores, MASKED)


def gather_weights(
    gain_one, qkv_weight, out_weight, gain_two, router_weight, expert_up, expert_down
):
    dense_set = (
        lax.all_gather(qkv_weight, ("fsdp", "tensor"), axis=0, tiled=True),
        lax.all_gather(out_weight, ("fsdp", "tensor"), axis=2, tiled=True),
        lax.all_gather(router_weight, ("fsdp", "tensor"), axis=0, tiled=True),
        lax.all_gather(gain_one, ("fsdp", "tensor"), axis=0, tiled=True),
        lax.all_gather(gain_two, ("fsdp", "tensor"), axis=0, tiled=True),
    )
    expert_set = (
        lax.all_gather(expert_up, "fsdp", axis=1, tiled=True),
        lax.all_gather(expert_down, "fsdp", axis=2, tiled=True),
    )
    return (dense_set, expert_set)


def reduce_expert_grads(up_grad, down_grad):
    return (
        lax.psum_scatter(up_grad, "fsdp", scatter_dimension=1, tiled=True),
        lax.psum_scatter(down_grad, "fsdp", scatter_dimension=2, tiled=True),
    )


def local(
    tokens,
    valid_mask,
    routes,
    teacher,
    gain_one,
    qkv_weight,
    out_weight,
    gain_two,
    router_weight,
    expert_up,
    expert_down,
):
    valid_total = lax.psum(jnp.sum(valid_mask.astype(jnp.float32)), ("fsdp", "tensor"))
    dense_set, expert_set = gather_weights(
        gain_one, qkv_weight, out_weight, gain_two, router_weight, expert_up, expert_down
    )
    qkv_full, output_complete, router_full, gain_a, gain_b = dense_set
    up_full, down_full = expert_set
    image_count, token_slots, model_width = tokens.shape
    head_dim = qkv_full.shape[2] // 3
    local_experts = expert_up.shape[0]
    tensor_size = lax.axis_size("tensor")
    group_images = image_count * tensor_size
    group_rows = group_images * token_slots
    top_choices = routes.shape[2]
    expert_count = local_experts * lax.axis_size("heads")
    capacity = 2 * top_choices * group_rows // expert_count
    slot_count = local_experts * capacity
    total_tokens = image_count * token_slots * lax.axis_size("fsdp") * tensor_size
    total_images = image_count * lax.axis_size("fsdp") * tensor_size
    score_scale = head_dim ** (-0.5)
    inputs = tokens.astype(jnp.float32)
    normed_one, spread_one = normalize(inputs)
    first_in = (normed_one * gain_a.astype(jnp.float32)).astype(jnp.bfloat16)
    projected = jnp.einsum(
        "isd,dhe->ishe", first_in, qkv_full, preferred_element_type=jnp.float32
    ).astype(jnp.bfloat16)
    queries = projected[..., :head_dim]
    key_rows = projected[..., head_dim : 2 * head_dim]
    values = projected[..., 2 * head_dim :]
    keys_ok = (valid_mask > 0)[:, None, None, :]
    scores = scores_of(queries, key_rows, keys_ok, score_scale)
    peak_score = jnp.max(scores, -1, keepdims=True)
    exp_scores = jnp.exp(scores - peak_score)
    score_total = jnp.sum(exp_scores, -1, keepdims=True)
    logarithm_total = peak_score + jnp.log(score_total)
    attention = (exp_scores / score_total).astype(jnp.bfloat16)
    combined_heads = jnp.einsum(
        "ihqk,ikhe->iqhe", attention, values, preferred_element_type=jnp.float32
    ).astype(jnp.bfloat16)
    attn_part = jnp.einsum(
        "iqhe,hed->iqd", combined_heads, output_complete, preferred_element_type=jnp.float32
    )
    attended = lax.psum(attn_part, "heads")
    residual = inputs + attended
    normed_two, spread_two = normalize(residual)
    second_in = (normed_two * gain_b.astype(jnp.float32)).astype(jnp.bfloat16)
    group_in = lax.all_gather(second_in, "tensor", axis=0, tiled=True)
    rows_in = group_in.reshape(group_rows, model_width)
    logits = jnp.dot(rows_in, router_full, preferred_element_type=jnp.float32)
    peak_logit = jnp.max(logits, -1, keepdims=True)
    exponent_logits = jnp.exp(logits - peak_logit)
    router_probs = exponent_logits / jnp.sum(exponent_logits, -1, keepdims=True)
    expert_ids = jnp.arange(expert_count, dtype=jnp.int32)
    route_pairs = routes.reshape(group_rows, top_choices)
    picked_hot = (route_pairs[:, :, None] == expert_ids[None, None, :]).astype(jnp.float32)
    gate_weight_values = jnp.sum(router_probs[:, None, :] * picked_hot, -1)
    flat_routes = route_pairs.reshape(group_rows * top_choices)
    route_hot = (flat_routes[:, None] == expert_ids[None, :]).astype(jnp.int32)
    earlier = jnp.cumsum(route_hot, 0) - route_hot
    slot_index = jnp.sum(earlier * route_hot, 1)
    first_expert = lax.axis_index("heads") * local_experts
    is_local = (flat_routes >= first_expert) & (flat_routes < first_expert + local_experts)
    target = jnp.where(is_local, (flat_routes - first_expert) * capacity + slot_index, slot_count)
    owner_row = jnp.arange(group_rows * top_choices, dtype=jnp.int32) // top_choices
    source = jnp.zeros((slot_count,), jnp.int32).at[target].set(owner_row, mode="drop")
    slot_gate = (
        jnp.zeros((slot_count,), jnp.float32)
        .at[target]
        .set(gate_weight_values.reshape(-1), mode="drop")
    )
    slot_pick = jnp.minimum(target, slot_count - 1)
    retain_mask = is_local.astype(jnp.float32)
    dispatched = rows_in[source].reshape(local_experts, capacity, model_width)
    before_gelu = jnp.einsum(
        "ecd,edf->ecf", dispatched, up_full, preferred_element_type=jnp.float32
    )
    hidden = jax.nn.gelu(before_gelu, approximate=False).astype(jnp.bfloat16)
    expert_out = jnp.einsum(
        "ecf,efd->ecd", hidden, down_full, preferred_element_type=jnp.float32
    ).reshape(slot_count, model_width)
    weighted = expert_out * slot_gate[:, None]
    moe_part = jnp.sum(
        (weighted[slot_pick] * retain_mask[:, None]).reshape(group_rows, top_choices, model_width),
        1,
    )
    moe_part = moe_part.reshape(group_images, token_slots, model_width)
    expert_sum = lax.psum(
        lax.psum_scatter(moe_part, "tensor", scatter_dimension=0, tiled=True), "heads"
    )
    final = residual + expert_sum
    valid_rows = valid_mask.astype(jnp.float32)[..., None]
    difference = (final - teacher.astype(jnp.float32)) * valid_rows
    loss_terms = jnp.sum(difference * difference, axis=(1, 2)) * (
        total_images / (valid_total * model_width)
    )
    final_grad = difference * (total_tokens / valid_total)
    dense_set, expert_set = gather_weights(
        gain_one, qkv_weight, out_weight, gain_two, router_weight, expert_up, expert_down
    )
    qkv_full, output_complete, router_full, gain_a, gain_b = dense_set
    up_full, down_full = expert_set
    moe_grad = final_grad.astype(jnp.bfloat16)
    group_grad = lax.all_gather(moe_grad, "tensor", axis=0, tiled=True).reshape(
        group_rows, model_width
    )
    slot_grad = group_grad[source].astype(jnp.float32)
    gate_slot_grad = jnp.sum(slot_grad * expert_out, -1)
    out_grad = (
        (slot_grad * slot_gate[:, None])
        .astype(jnp.bfloat16)
        .reshape(local_experts, capacity, model_width)
    )
    expert_down_grad = jnp.einsum(
        "ecf,ecd->efd", hidden, out_grad, preferred_element_type=jnp.float32
    )
    hidden_grad = jnp.einsum(
        "ecd,efd->ecf", out_grad, down_full, preferred_element_type=jnp.float32
    )
    normal_cdf = 0.5 * (1.0 + lax.erf(before_gelu * ROOT_HALF))
    slope = normal_cdf + before_gelu * DENSITY * jnp.exp(-0.5 * before_gelu * before_gelu)
    pre_grad = (hidden_grad * slope).astype(jnp.bfloat16)
    expert_up_grad = jnp.einsum(
        "ecd,ecf->edf", dispatched, pre_grad, preferred_element_type=jnp.float32
    )
    row_grad = jnp.einsum(
        "ecf,edf->ecd", pre_grad, up_full, preferred_element_type=jnp.float32
    ).reshape(slot_count, model_width)
    rows_part = jnp.sum(
        (row_grad[slot_pick] * retain_mask[:, None]).reshape(group_rows, top_choices, model_width),
        1,
    )
    rows_part = rows_part.reshape(group_images, token_slots, model_width)
    gate_part = (gate_slot_grad[slot_pick] * retain_mask).reshape(
        group_images, token_slots, top_choices
    )
    rows_share, gate_share = (
        lax.psum_scatter(rows_part, "tensor", scatter_dimension=0, tiled=True),
        lax.psum_scatter(gate_part, "tensor", scatter_dimension=0, tiled=True),
    )
    second_grad, gate_grad = lax.psum((rows_share, gate_share), "heads")
    own_start = lax.axis_index("tensor") * image_count * token_slots
    own_rows = image_count * token_slots
    own_probs = lax.dynamic_slice_in_dim(router_probs, own_start, own_rows, 0).reshape(
        image_count, token_slots, expert_count
    )
    own_hot = lax.dynamic_slice_in_dim(picked_hot, own_start, own_rows, 0).reshape(
        image_count, token_slots, top_choices, expert_count
    )
    prob_grad = jnp.sum(gate_grad[..., None] * own_hot, 2)
    logit_grad = (
        own_probs * (prob_grad - jnp.sum(own_probs * prob_grad, -1, keepdims=True))
    ).astype(jnp.bfloat16)
    router_grad = jnp.einsum(
        "isd,ise->de", second_in, logit_grad, preferred_element_type=jnp.float32
    )
    second_grad = second_grad + jnp.einsum(
        "ise,de->isd", logit_grad, router_full, preferred_element_type=jnp.float32
    )
    residual_norm, gain_two_grad = norm_back(
        second_grad, normed_two, spread_two, gain_b.astype(jnp.float32)
    )
    residual_grad = final_grad + residual_norm
    attended_output_gradient = residual_grad.astype(jnp.bfloat16)
    out_weight_grad = jnp.einsum(
        "iqhe,iqd->hed",
        combined_heads,
        attended_output_gradient,
        preferred_element_type=jnp.float32,
    )
    mixed_grad = jnp.einsum(
        "iqd,hed->iqhe",
        attended_output_gradient,
        output_complete,
        preferred_element_type=jnp.float32,
    ).astype(jnp.bfloat16)
    scores = scores_of(queries, key_rows, keys_ok, score_scale)
    probs = jnp.exp(scores - logarithm_total)
    probs_low = probs.astype(jnp.bfloat16)
    prob_part = jnp.einsum(
        "iqhe,ikhe->ihqk", mixed_grad, values, preferred_element_type=jnp.float32
    )
    score_grad = (probs * (prob_part - jnp.sum(probs * prob_part, -1, keepdims=True))).astype(
        jnp.bfloat16
    )
    query_grad = (
        jnp.einsum("ihqk,ikhe->iqhe", score_grad, key_rows, preferred_element_type=jnp.float32)
        * score_scale
    )
    key_grad = (
        jnp.einsum("ihqk,iqhe->ikhe", score_grad, queries, preferred_element_type=jnp.float32)
        * score_scale
    )
    value_grad = jnp.einsum(
        "ihqk,iqhe->ikhe", probs_low, mixed_grad, preferred_element_type=jnp.float32
    )
    projected_grad = jnp.concatenate([query_grad, key_grad, value_grad], -1).astype(jnp.bfloat16)
    qkv_grad = jnp.einsum(
        "isd,ishe->dhe", first_in, projected_grad, preferred_element_type=jnp.float32
    )
    first_part = jnp.einsum(
        "ishe,dhe->isd", projected_grad, qkv_full, preferred_element_type=jnp.float32
    )
    first_grad = lax.psum(first_part, "heads")
    input_norm, gain_one_grad = norm_back(
        first_grad, normed_one, spread_one, gain_a.astype(jnp.float32)
    )
    tokens_grad = residual_grad + input_norm
    dense_grads = (
        lax.psum_scatter(qkv_grad, ("fsdp", "tensor"), scatter_dimension=0, tiled=True),
        lax.psum_scatter(out_weight_grad, ("fsdp", "tensor"), scatter_dimension=2, tiled=True),
        lax.psum_scatter(router_grad, ("fsdp", "tensor"), scatter_dimension=0, tiled=True),
        lax.psum_scatter(gain_one_grad, ("fsdp", "tensor"), scatter_dimension=0, tiled=True),
        lax.psum_scatter(gain_two_grad, ("fsdp", "tensor"), scatter_dimension=0, tiled=True),
    )
    expert_grads = reduce_expert_grads(expert_up_grad, expert_down_grad)
    return (
        final.astype(jnp.bfloat16),
        loss_terms,
        tokens_grad,
        dense_grads[3],
        dense_grads[0],
        dense_grads[1],
        dense_grads[4],
        dense_grads[2],
        expert_grads[0],
        expert_grads[1],
    )


def solution(mesh):
    in_specs = (
        P(("fsdp", "tensor"), None, None),
        P(("fsdp", "tensor"), None),
        P("fsdp", None, None),
        P(("fsdp", "tensor"), None, None),
        P(("fsdp", "tensor")),
        P(("fsdp", "tensor"), "heads", None),
        P("heads", None, ("fsdp", "tensor")),
        P(("fsdp", "tensor")),
        P(("fsdp", "tensor"), None),
        P("heads", "fsdp", "tensor"),
        P("heads", "tensor", "fsdp"),
    )
    out_specs = (
        P(("fsdp", "tensor"), None, None),
        P(("fsdp", "tensor")),
        P(("fsdp", "tensor"), None, None),
        P(("fsdp", "tensor")),
        P(("fsdp", "tensor"), "heads", None),
        P("heads", None, ("fsdp", "tensor")),
        P(("fsdp", "tensor")),
        P(("fsdp", "tensor"), None),
        P("heads", "fsdp", "tensor"),
        P("heads", "tensor", "fsdp"),
    )
    return jax.shard_map(local, mesh=mesh, in_specs=in_specs, out_specs=out_specs, check_vma=False)
```

profile of v0, /device:TPU:0, one launch (start us, length us, event | category | flops | bytes accessed | tf_op | source)
XLA Modules:
  0.0 1239.2 jit_solution(9188463020650189161)
XLA Ops:
  7.3 1.1 copy.139
  8.4 14.6 %all_gather.35 = bf16[768,3,192]{2,1,0:T(4,128)(2,1)S(1)} all-gather(bf16[96,3,192]{2,1,0:T(4,128)(2,1)S(1)} %copy.139), channel_id=1, replica_groups=mesh['fsdp'=2,'heads'=4,'tensor'=4] {'fsdp','tensor'}, dimensions={0}, use_global_device_ids=true | all-gather | bytes 995328 | tf_op jit(solution)/shard_map/all_gather | solution.py:41
  25.8 13.2 %all-reduce.6 = (bf16[768]{0:T(1024)(128)(2,1)S(1)}, bf16[768]{0:T(1024)(128)(2,1)S(1)}) all-reduce(bf16[768]{0:T(1024)(128)(2,1)S(1)} %dynamic-update-slice, bf16[768]{0:T(1024)(128)(2,1)S(1)} %dynamic-update-slice.1), channel_id=1, replica_groups=mesh['fsdp'=2,'heads'=4,'tensor'=4] {'fsdp','tensor'}, use_global_device_ids=true, to_apply=%add | all-reduce | flops 1536 | bytes 6144
  42.2 9.4 all_gather.36
  52.1 1.2 convolution_bitcast_fusion.2
  53.4 44.1 %all-reduce.12.cloned.1.call-done = f32[1,256,768]{2,1,0:T(8,128)} async-done(((f32[1,256,768]{2,1,0:T(8,128)}), f32[1,256,768]{2,1,0:T(8,128)}) %all-reduce.12.cloned.1.call-update) | async-done | bytes 786448 | tf_op jit(solution)/shard_map/psum | solution.py:115
  97.5 1.3 fusion.76
  99.7 1.0 multiply_convert_fusion.1
  104.2 9.1 reduce-window.6
  113.8 9.2 all-gather
  123.8 1.0 copy.156
  125.1 8.0 scatter_custom_fusion
  133.8 6.4 gather_fusion
  140.3 1.4 fusion.79
  143.0 8.6 scatter_custom_fusion.1
  151.7 87.8 %all-gather.8.cloned.1.call-done = bf16[8,768,768]{2,1,0:T(8,128)(2,1)} async-done(((bf16[8,384,768]{2,1,0:T(8,128)(2,1)}), bf16[8,768,768]{2,1,0:T(8,128)(2,1)}) %all-gather.8.cloned.1.call-update) | async-done | bytes 9437200 | tf_op jit(solution)/shard_map/all_gather | solution.py:48
  239.5 6.1 fusion.41
  245.6 1.6 copy-done.22
  247.2 7.1 fusion.4
  254.3 104.6 %all-gather.10.cloned.1.call-done = bf16[8,768,768]{2,1,0:T(8,128)(2,1)} async-done(((bf16[8,768,384]{2,1,0:T(8,128)(2,1)}), bf16[8,768,768]{2,1,0:T(8,128)(2,1)}) %all-gather.10.cloned.1.call-update) | async-done | bytes 9437200 | tf_op jit(solution)/shard_map/all_gather | solution.py:49
  359.0 5.1 fusion.80
  364.1 1.7 copy-done.1
  366.0 10.2 gather_fusion.1
  376.2 8.2 gather.23
  384.4 11.2 multiply_reduce_fusion.1
  395.7 38.0 %reduce-scatter.12.cloned.1.call-done = f32[1,256,768]{2,1,0:T(8,128)} async-done(((f32[4,256,768]{2,1,0:T(8,128)}), f32[1,256,768]{2,1,0:T(8,128)}) %reduce-scatter.12.cloned.1.call-update) | async-done | bytes 786448 | tf_op jit(solution)/shard_map/reduce_scatter | solution.py:160
  434.4 13.3 %psum.44 = f32[]{:T(128)} all-reduce(f32[]{:T(128)} %convert_reduce_fusion.1), channel_id=1, replica_groups=mesh['fsdp'=2,'heads'=4,'tensor'=4] {'fsdp','tensor'}, use_global_device_ids=true, to_apply=%region_20.21 | all-reduce | flops 1 | bytes 8 | tf_op jit(solution)/shard_map/psum | solution.py:74
  448.4 31.4 %all-reduce.14.cloned.1.call-done = f32[1,256,768]{2,1,0:T(8,128)} async-done(((f32[1,256,768]{2,1,0:T(8,128)}), f32[1,256,768]{2,1,0:T(8,128)}) %all-reduce.14.cloned.1.call-update) | async-done | bytes 786448 | tf_op jit(solution)/shard_map/psum | solution.py:159
  479.7 2.4 multiply_convert_fusion.2
  482.4 18.9 %all-gather.12.cloned.1.call-done = bf16[4,256,768]{2,1,0:T(8,128)(2,1)} async-done(((bf16[1,256,768]{2,1,0:T(8,128)(2,1)}), bf16[4,256,768]{2,1,0:T(8,128)(2,1)}) %all-gather.12.cloned.1.call-update) | async-done | bytes 1572880 | tf_op jit(solution)/shard_map/all_gather | solution.py:175
  501.3 6.1 gather_fusion.2
  507.5 1.2 copy-done.10
  508.6 6.4 fusion.9
  515.0 7.3 fusion.81
  522.4 10.2 gather_fusion.3
  532.5 8.2 gather.26
  540.7 11.2 multiply_reduce_fusion
  554.5 1.8 fusion.1
  556.3 9.7 gather_fusion.4
  566.8 6.0 all-reduce.2
  572.8 17.3 %reduce-scatter.14.cloned.1.call-done = f32[1,256,768]{2,1,0:T(8,128)} async-done(((f32[4,256,768]{2,1,0:T(8,128)}), f32[1,256,768]{2,1,0:T(8,128)}) %reduce-scatter.14.cloned.1.call-update) | async-done | bytes 786448 | tf_op jit(solution)/shard_map/reduce_scatter | solution.py:209
  590.8 11.7 psum.46
  603.4 1.1 fusion.47
  604.5 31.7 %all-reduce.16.cloned.1.call-done = f32[1,256,768]{2,1,0:T(8,128)} async-done(((f32[1,256,768]{2,1,0:T(8,128)}), f32[1,256,768]{2,1,0:T(8,128)}) %all-reduce.16.cloned.1.call-update) | async-done | bytes 786448 | tf_op jit(solution)/shard_map/psum | solution.py:212
  636.2 2.3 multiply_reduce_fusion.2
  638.5 1.7 multiply_add_fusion
  640.2 1.4 convolution_convert_fusion.1
  643.0 1.4 convolution_bitcast_fusion
  645.7 1.7 reshape.523
  647.5 3.2 fusion.45
  650.8 8.0 fusion.82
  658.9 1.3 copy-done.9
  660.7 8.0 fusion.16
  670.1 2.3 reduce-scatter.24.cloned.1.call-done
  672.4 1.5 copy.179
  674.5 43.9 %all-reduce.18.cloned.1.call-done = f32[1,256,768]{2,1,0:T(8,128)} async-done(((f32[1,256,768]{2,1,0:T(8,128)}), f32[1,256,768]{2,1,0:T(8,128)}) %all-reduce.18.cloned.1.call-update) | async-done | bytes 786448 | tf_op jit(solution)/shard_map/psum | solution.py:275
  718.5 1.5 fusion.38
  720.0 13.8 %all-reduce.5 = (f32[768]{0:T(1024)S(1)}, f32[768]{0:T(1024)S(1)}) all-reduce(f32[768]{0:T(1024)S(1)} %get-tuple-element.14, f32[768]{0:T(1024)S(1)} %copy-done.57), channel_id=5, replica_groups=mesh['fsdp'=2,'heads'=4,'tensor'=4] {'fsdp','tensor'}, use_global_device_ids=true, to_apply=%region_36.37.clone | all-reduce | flops 1536 | bytes 12288
  735.0 2.3 fusion.37
  737.3 18.5 %reduce-scatter.22.cloned.1.call-done = f32[96,192]{1,0:T(8,128)} async-done(((f32[768,192]{1,0:T(8,128)}), f32[96,192]{1,0:T(8,128)}) %reduce-scatter.22.cloned.1.call-update) | async-done | bytes 73744
  755.8 1.0 reshape.524
  757.6 44.6 %reduce-scatter.16.cloned.1.call-done = f32[96,3,192]{2,0,1:T(8,128)} async-done(((f32[768,3,192]{2,0,1:T(8,128)}), f32[96,3,192]{2,0,1:T(8,128)}) %reduce-scatter.16.cloned.1.call-update) | async-done | bytes 221200 | tf_op jit(solution)/shard_map/reduce_scatter | solution.py:281
  802.2 214.5 %reduce-scatter.18.cloned.1.call-done = f32[8,384,768]{2,1,0:T(8,128)} async-done(((f32[8,768,768]{2,1,0:T(8,128)}), f32[8,384,768]{2,1,0:T(8,128)}) %reduce-scatter.18.cloned.1.call-update) | async-done | bytes 9437200 | tf_op jit(solution)/shard_map/reduce_scatter | solution.py:56
  1016.8 214.5 %reduce-scatter.20.cloned.1.call-done = f32[8,768,384]{2,1,0:T(8,128)} async-done(((f32[8,768,768]{2,1,0:T(8,128)}), f32[8,768,384]{2,1,0:T(8,128)}) %reduce-scatter.20.cloned.1.call-update) | async-done | bytes 9437200 | tf_op jit(solution)/shard_map/reduce_scatter | solution.py:57
  (236 shorter events, 24.7 us)
Async XLA Ops:
  7.2 16.8 %copy-start.60 = (u32[32]{0:T(128)S(1)}, u32[32]{0:T(128)}, u32[]{:S(2)}) copy-start(u32[32]{0:T(128)} %constant.143) | copy-start | bytes 388
  7.2 18.1 %copy-start.63 = (bf16[96]{0:T(256)(128)(2,1)S(1)}, bf16[96]{0:T(256)(128)(2,1)}, u32[]{:S(2)}) copy-start(bf16[96]{0:T(256)(128)(2,1)} %param.15) | copy-start | bytes 580
  7.2 18.4 %copy-start.64 = (bf16[96]{0:T(256)(128)(2,1)S(1)}, bf16[96]{0:T(256)(128)(2,1)}, u32[]{:S(2)}) copy-start(bf16[96]{0:T(256)(128)(2,1)} %param.18) | copy-start | bytes 580
  7.2 31.8 %copy-start.12 = (bf16[1,256,768]{2,1,0:T(8,128)(2,1)S(1)}, bf16[1,256,768]{2,1,0:T(8,128)(2,1)}, u32[]{:S(2)}) copy-start(bf16[1,256,768]{2,1,0:T(8,128)(2,1)} %param.11) | copy-start | bytes 1179652
  7.2 90.3 %all-reduce.12.cloned.1.call-start = ((), (), s32[]{:S(2)}) async-start(), calls=%async_computation.7 | async-start | bytes 1572864 | tf_op jit(solution)/shard_map/psum | solution.py:115
  23.0 17.5 %copy-start.61 = (s32[1,256]{1,0:T(1,128)S(1)}, s32[1,256]{1,0:T(1,128)}, u32[]{:S(2)}) copy-start(s32[1,256]{1,0:T(1,128)} %param.12) | copy-start | bytes 3076
  23.9 18.2 %copy-start.27 = (bf16[768,3,192]{0,2,1:T(8,128)(2,1)}, bf16[768,3,192]{0,2,1:T(8,128)(2,1)S(1)}, u32[]{:S(2)}) copy-start(bf16[768,3,192]{0,2,1:T(8,128)(2,1)S(1)} %copy.140) | copy-start | bytes 2654212
  39.0 3.1 copy-start.39
  41.8 11.5 copy-start.56
  42.1 57.0 %copy-start.33 = (bf16[256,3,64]{0,2,1:T(8,128)(2,1)}, bf16[256,3,64]{0,2,1:T(8,128)(2,1)S(1)}, u32[]{:S(2)}) copy-start(bf16[256,3,64]{0,2,1:T(8,128)(2,1)S(1)} %fusion.25) | copy-start | bytes 294916
  52.1 48.6 %copy-start.24 = (bf16[3,64,768]{2,1,0:T(8,128)(2,1)}, bf16[3,64,768]{2,1,0:T(8,128)(2,1)S(1)}, u32[]{:S(2)}) copy-start(bf16[3,64,768]{2,1,0:T(8,128)(2,1)S(1)} %copy.143) | copy-start | bytes 884740
  53.3 80.5 %all-gather.6.cloned.1.call-start = ((), (), s32[]{:S(2)}) async-start(), calls=%async_computation.8 | async-start | bytes 1966080 | tf_op jit(solution)/shard_map/all_gather | solution.py:119
  53.4 48.1 %copy-start.41 = (f32[768]{0:T(1024)}, f32[768]{0:T(1024)S(1)}, u32[]{:S(2)}) copy-start(f32[768]{0:T(1024)S(1)} %convert_element_type.117) | copy-start | bytes 9220
  98.8 2.6 copy-start.50
  100.7 138.8 %all-gather.8.cloned.1.call-start = ((), (), s32[]{:S(2)}) async-start(), calls=%async_computation.9 | async-start | bytes 14155776 | tf_op jit(solution)/shard_map/all_gather | solution.py:48
  101.5 257.5 %all-gather.10.cloned.1.call-start = ((), (), s32[]{:S(2)}) async-start(), calls=%async_computation.10 | async-start | bytes 14155776 | tf_op jit(solution)/shard_map/all_gather | solution.py:49
  102.0 11.8 copy-start.58
  102.1 331.6 %reduce-scatter.12.cloned.1.call-start = ((), (), s32[]{:S(2)}) async-start(), calls=%async_computation.11 | async-start | bytes 3932160 | tf_op jit(solution)/shard_map/reduce_scatter | solution.py:160
  125.1 8.7 copy-start.59
  133.2 7.1 copy-start.46
  133.8 6.5 copy-start
  140.3 105.3 %copy-start.17 = (bf16[1024,768]{1,0:T(8,128)(2,1)}, bf16[1024,768]{1,0:T(8,128)(2,1)S(1)}, u32[]{:S(2)}) copy-start(bf16[1024,768]{1,0:T(8,128)(2,1)S(1)} %gather_fusion) | copy-start | bytes 4718596
  151.7 355.8 %copy-start.44 = (f32[1024]{0:T(1024)}, f32[1024]{0:T(1024)S(1)}, u32[]{:S(2)}) copy-start(f32[1024]{0:T(1024)S(1)} %scatter_custom_fusion.1) | copy-start | bytes 12292
  254.3 104.6 %copy-start.8 = (bf16[8,128,768]{2,1,0:T(8,128)(2,1)}, bf16[8,128,768]{2,1,0:T(8,128)(2,1)S(1)}, u32[]{:S(2)}) copy-start(bf16[8,128,768]{2,1,0:T(8,128)(2,1)S(1)} %fusion.4) | copy-start | bytes 4718596
  376.2 8.2 copy-start.19
  395.6 38.2 %copy-start.62 = (s32[1,256]{1,0:T(1,128)S(1)}, s32[1,256]{1,0:T(1,128)}, u32[]{:S(2)}) copy-start(s32[1,256]{1,0:T(1,128)} %param.12) | copy-start | bytes 3076
  395.6 84.2 %copy-start.4 = (f32[1,256,768]{2,1,0:T(8,128)S(1)}, f32[1,256,768]{2,1,0:T(8,128)}, u32[]{:S(2)}) copy-start(f32[1,256,768]{2,1,0:T(8,128)} %copy-done.3) | copy-start | bytes 2359300
  395.6 84.2 %copy-start.35 = (bf16[1,256,768]{2,1,0:T(8,128)(2,1)S(1)}, bf16[1,256,768]{2,1,0:T(8,128)(2,1)}, u32[]{:S(2)}) copy-start(bf16[1,256,768]{2,1,0:T(8,128)(2,1)} %param.14) | copy-start | bytes 1179652
  395.6 105.8 %copy-start.47 = (s32[1024]{0:T(1024)S(1)}, s32[1024]{0:T(1024)}, u32[]{:S(2)}) copy-start(s32[1024]{0:T(1024)} %copy-done.46) | copy-start | bytes 12292
  395.6 84.1 %all-reduce.14.cloned.1.call-start = ((), (), s32[]{:S(2)}) async-start(), calls=%async_computation.12 | async-start | bytes 1572864 | tf_op jit(solution)/shard_map/psum | solution.py:159
  433.7 67.6 %all-gather.12.cloned.1.call-start = ((), (), s32[]{:S(2)}) async-start(), calls=%async_computation.13 | async-start | bytes 1966080 | tf_op jit(solution)/shard_map/all_gather | solution.py:175
  482.2 107.9 %reduce-scatter.14.cloned.1.call-start = ((), (), s32[]{:S(2)}) async-start(), calls=%async_computation.14 | async-start | bytes 3932160 | tf_op jit(solution)/shard_map/reduce_scatter | solution.py:209
  515.0 7.3 copy-start.15
  532.5 8.2 copy-start.20
  551.9 2.6 copy-start.2
  552.0 84.3 %all-reduce.16.cloned.1.call-start = ((), (), s32[]{:S(2)}) async-start(), calls=%async_computation.15 | async-start | bytes 1572864 | tf_op jit(solution)/shard_map/psum | solution.py:212
  556.3 47.0 %copy-start.30 = (f32[1024,32]{0,1:T(8,128)S(1)}, f32[1024,32]{0,1:T(8,128)}, u32[]{:S(2)}) copy-start(f32[1024,32]{0,1:T(8,128)} %copy-done.29) | copy-start | bytes 393220
  556.3 47.0 %copy-start.21 = (bf16[1,256,768]{2,1,0:T(8,128)(2,1)S(1)}, bf16[1,256,768]{2,1,0:T(8,128)(2,1)}, u32[]{:S(2)}) copy-start(bf16[1,256,768]{2,1,0:T(8,128)(2,1)} %multiply_convert_fusion.1) | copy-start | bytes 1179652
  566.0 70.2 %copy-start.5 = (f32[1,256,768]{2,1,0:T(8,128)S(1)}, f32[1,256,768]{2,1,0:T(8,128)}, u32[]{:S(2)}) copy-start(f32[1,256,768]{2,1,0:T(8,128)} %copy-done.3) | copy-start | bytes 2359300
  566.0 70.2 %copy-start.31 = (bf16[768,32]{0,1:T(8,128)(2,1)S(1)}, bf16[768,32]{0,1:T(8,128)(2,1)}, u32[]{:S(2)}) copy-start(bf16[768,32]{0,1:T(8,128)(2,1)} %reshape.512) | copy-start | bytes 147460
  566.1 70.2 %copy-start.42 = (f32[768]{0:T(1024)S(1)}, f32[768]{0:T(1024)}, u32[]{:S(2)}) copy-start(f32[768]{0:T(1024)} %copy-done.41) | copy-start | bytes 9220
  566.1 70.2 %copy-start.51 = (f32[256]{0:T(256)S(1)}, f32[256]{0:T(256)}, u32[]{:S(2)}) copy-start(f32[256]{0:T(256)} %copy-done.50) | copy-start | bytes 3076
  566.1 70.2 %copy-start.55 = (f32[256]{0:T(256)S(1)}, f32[256]{0:T(256)}, u32[]{:S(2)}) copy-start(f32[256]{0:T(256)} %copy-done.54) | copy-start | bytes 3076
  566.1 72.4 %copy-start.23 = (f32[1,256,768]{2,1,0:T(8,128)S(1)}, f32[1,256,768]{2,1,0:T(8,128)}, u32[]{:S(2)}) copy-start(f32[1,256,768]{2,1,0:T(8,128)} %get-tuple-element.23) | copy-start | bytes 2359300
  590.1 82.3 %reduce-scatter.24.cloned.1.call-start = ((), (), s32[]{:S(2)}) async-start(), calls=%async_computation.21 | async-start | bytes 442368
  604.5 37.2 %copy-start.7 = (f32[3,256,256]{1,2,0:T(8,128)S(1)}, f32[3,256,256]{1,2,0:T(8,128)}, u32[]{:S(2)}) copy-start(f32[3,256,256]{1,2,0:T(8,128)} %copy-done.6) | copy-start | bytes 2359300
  604.5 114.0 %all-reduce.18.cloned.1.call-start = ((), (), s32[]{:S(2)}) async-start(), calls=%async_computation.16 | async-start | bytes 1572864 | tf_op jit(solution)/shard_map/psum | solution.py:275
  638.5 3.4 copy-start.26
  640.2 4.5 copy-start.13
  641.9 2.4 copy-start.38
  642.3 2.4 copy-start.34
  642.7 3.0 copy-start.36
  644.4 3.1 copy-start.40
  644.4 3.1 copy-start.49
  644.4 3.1 copy-start.53
  644.4 111.4 %reduce-scatter.22.cloned.1.call-start = ((), (), s32[]{:S(2)}) async-start(), calls=%async_computation.20 | async-start | bytes 884736
  647.4 3.4 copy-start.16
  647.4 3.4 copy-start.18
  647.5 154.8 %reduce-scatter.16.cloned.1.call-start = ((), (), s32[]{:S(2)}) async-start(), calls=%async_computation.17 | async-start | bytes 2654208 | tf_op jit(solution)/shard_map/reduce_scatter | solution.py:281
  650.8 366.0 %reduce-scatter.18.cloned.1.call-start = ((), (), s32[]{:S(2)}) async-start(), calls=%async_computation.18 | async-start | bytes 28311552 | tf_op jit(solution)/shard_map/reduce_scatter | solution.py:56
  658.8 1.9 copy-start.45
  658.8 572.4 %reduce-scatter.20.cloned.1.call-start = ((), (), s32[]{:S(2)}) async-start(), calls=%async_computation.19 | async-start | bytes 28311552 | tf_op jit(solution)/shard_map/reduce_scatter | solution.py:57
  668.7 51.3 %copy-start.57 = (f32[768]{0:T(1024)S(1)}, f32[768]{0:T(1024)}, u32[]{:S(2)}) copy-start(f32[768]{0:T(1024)} %get-tuple-element.12) | copy-start | bytes 9220
  668.7 66.3 %copy-start.14 = (f32[1,256,768]{2,1,0:T(8,128)S(1)}, f32[1,256,768]{2,1,0:T(8,128)}, u32[]{:S(2)}) copy-start(f32[1,256,768]{2,1,0:T(8,128)} %copy-done.13) | copy-start | bytes 2359300
  (17 other events, 19.5 us)
Sparse Core Ops, SparseCore 0:
  53.4 44.0 all-reduce.11
  100.8 18.9 all-gather.5
  121.4 118.0 all-gather.7
  240.9 117.9 all-gather.9
  395.7 37.9 reduce-scatter.11
  436.0 43.6 all-reduce.13
  482.3 18.9 all-gather.11
  552.1 37.9 reduce-scatter.13
  592.5 43.6 all-reduce.15
  639.1 33.2 reduce-scatter.23
  674.8 43.6 all-reduce.17
  721.5 34.2 reduce-scatter.21
  759.7 42.4 reduce-scatter.15
  805.1 211.6 reduce-scatter.17
  1019.6 211.6 reduce-scatter.19
where the time goes:
time: 1250 us; the launch traced here: 1240 us
  waiting for transfers between devices  914 us (73%)
  local copies, waits for them, and re-layouts  102 us (8%)
  blocking collectives  91.2 us (7%)
  other arithmetic  55.8 us (4%)
  matrix products  55.2 us (4%)
  between operations  19.8 us (2%)
    reduce_scatter x1, waiting for transfers between devices, reduce_expert_grads(): lax.psum_scatter(up_grad, 'fsdp', scatter_dimension=1, tiled=True)  215 us
    reduce_scatter x1, waiting for transfers between devices, reduce_expert_grads(): lax.psum_scatter(down_grad, 'fsdp', scatter_dimension=2, tiled=True)  215 us
    all_gather x1, waiting for transfers between devices, gather_weights(): lax.all_gather(expert_down, 'fsdp', axis=2, tiled=True)  105 us
    all_gather x1, waiting for transfers between devices, gather_weights(): lax.all_gather(expert_up, 'fsdp', axis=1, tiled=True)  87.8 us
    reduce_scatter x1, waiting for transfers between devices, local(): lax.psum_scatter(qkv_grad, ('fsdp', 'tensor'), scatter_dimension=0, tiled...  44.6 us
    psum x1, waiting for transfers between devices, local(): attended = lax.psum(attn_part, 'heads')  44.1 us
    psum x1, waiting for transfers between devices, local(): first_grad = lax.psum(first_part, 'heads')  43.9 us
    reduce_scatter x1, waiting for transfers between devices, local(): lax.psum_scatter(moe_part, 'tensor', scatter_dimension=0, tiled=True)  38 us
  transfers between devices with their start and end apart: 15, of which 14 were waited for; matrix products, arithmetic and copies ran while one was open for 9% of the time, Pallas kernels for 0%

commit v1 on v0

--- a/solution.py
+++ b/solution.py
@@ -272,7 +272,11 @@
     first_part = jnp.einsum(
         "ishe,dhe->isd", projected_grad, qkv_full, preferred_element_type=jnp.float32
     )
-    first_grad = lax.psum(first_part, "heads")
+    first_grad = first_part
+    for hop in (1, 2):
+        first_grad = first_grad + lax.ppermute(
+            first_grad, "heads", [(dev, dev ^ hop) for dev in range(4)]
+        )
     input_norm, gain_one_grad = norm_back(
         first_grad, normed_one, spread_one, gain_a.astype(jnp.float32)
     )

time: 1250 us -> 1200 us (0.960)
  waiting for transfers between devices: 914 us -> 860 us
    psum x1 -> x0, waiting for transfers between devices: 43.9 us -> none  [local(): first_grad = lax.psum(first_part, 'heads')]
    reduce_scatter x1, waiting for transfers between devices: 44.6 us -> 8.27 us  [local(): lax.psum_scatter(qkv_grad, ('fsdp', 'tensor'), scatter_dimension=0, tiled...]
    ppermute x0 -> x2, waiting for transfers between devices: none -> 35.8 us  [local(): lax.ppermute(first_grad, 'heads', [(dev, dev ^ hop) for dev in range(4)])]
  transfers between devices with their start and end apart: 15 -> 16, of which waited for: 14 -> 14; matrix products, arithmetic and copies ran while one was open for 9% -> 9% of each run, Pallas kernels for 0% -> 0%
where the time goes in v1:
time: 1200 us; the launch traced here: 1190 us
  waiting for transfers between devices  860 us (72%)
  local copies, waits for them, and re-layouts  105 us (9%)
  blocking collectives  91.4 us (8%)
  matrix products  59.1 us (5%)
  other arithmetic  55.5 us (5%)
  between operations  19.7 us (2%)
    reduce_scatter x1, waiting for transfers between devices, reduce_expert_grads(): lax.psum_scatter(up_grad, 'fsdp', scatter_dimension=1, tiled=True)  215 us
    reduce_scatter x1, waiting for transfers between devices, reduce_expert_grads(): lax.psum_scatter(down_grad, 'fsdp', scatter_dimension=2, tiled=True)  215 us
    all_gather x1, waiting for transfers between devices, gather_weights(): lax.all_gather(expert_down, 'fsdp', axis=2, tiled=True)  105 us
    all_gather x1, waiting for transfers between devices, gather_weights(): lax.all_gather(expert_up, 'fsdp', axis=1, tiled=True)  87.8 us
    psum x1, waiting for transfers between devices, local(): attended = lax.psum(attn_part, 'heads')  44.1 us
    reduce_scatter x1, waiting for transfers between devices, local(): lax.psum_scatter(moe_part, 'tensor', scatter_dimension=0, tiled=True)  38 us
    ppermute x2, waiting for transfers between devices, local(): lax.ppermute(first_grad, 'heads', [(dev, dev ^ hop) for dev in range(4)])  35.8 us
    unnamed x3, blocking collectives  33.2 us
  transfers between devices with their start and end apart: 16, of which 14 were waited for; matrix products, arithmetic and copies ran while one was open for 9% of the time, Pallas kernels for 0%

profile of v1, /device:TPU:0, one launch (start us, length us, event | category | flops | bytes accessed | tf_op | source)
XLA Modules:
  0.0 1194.2 jit_solution(9269272417598960800)
XLA Ops:
  7.3 1.1 copy.139
  8.4 14.6 %all_gather.35 = bf16[768,3,192]{2,1,0:T(4,128)(2,1)S(1)} all-gather(bf16[96,3,192]{2,1,0:T(4,128)(2,1)S(1)} %copy.139), channel_id=1, replica_groups=mesh['fsdp'=2,'heads'=4,'tensor'=4] {'fsdp','tensor'}, dimensions={0}, use_global_device_ids=true | all-gather | bytes 995328 | tf_op jit(solution)/shard_map/all_gather | solution.py:41
  25.8 13.2 %all-reduce.6 = (bf16[768]{0:T(1024)(128)(2,1)S(1)}, bf16[768]{0:T(1024)(128)(2,1)S(1)}) all-reduce(bf16[768]{0:T(1024)(128)(2,1)S(1)} %dynamic-update-slice, bf16[768]{0:T(1024)(128)(2,1)S(1)} %dynamic-update-slice.1), channel_id=1, replica_groups=mesh['fsdp'=2,'heads'=4,'tensor'=4] {'fsdp','tensor'}, use_global_device_ids=true, to_apply=%add | all-reduce | flops 1536 | bytes 6144
  42.3 9.4 all_gather.36
  52.2 1.2 convolution_bitcast_fusion.2
  53.5 44.1 %all-reduce.11.cloned.1.call-done = f32[1,256,768]{2,1,0:T(8,128)} async-done(((f32[1,256,768]{2,1,0:T(8,128)}), f32[1,256,768]{2,1,0:T(8,128)}) %all-reduce.11.cloned.1.call-update) | async-done | bytes 786448 | tf_op jit(solution)/shard_map/psum | solution.py:115
  97.6 1.3 fusion.76
  104.3 9.1 reduce-window.6
  113.9 9.2 all-gather
  125.2 8.0 scatter_custom_fusion
  133.9 6.4 gather_fusion
  140.4 1.4 fusion.79
  143.1 8.6 scatter_custom_fusion.1
  151.8 87.8 %all-gather.8.cloned.1.call-done = bf16[8,768,768]{2,1,0:T(8,128)(2,1)} async-done(((bf16[8,384,768]{2,1,0:T(8,128)(2,1)}), bf16[8,768,768]{2,1,0:T(8,128)(2,1)}) %all-gather.8.cloned.1.call-update) | async-done | bytes 9437200 | tf_op jit(solution)/shard_map/all_gather | solution.py:48
  239.6 6.1 fusion.41
  245.7 1.6 copy-done.21
  247.3 7.1 fusion.4
  254.4 104.6 %all-gather.10.cloned.1.call-done = bf16[8,768,768]{2,1,0:T(8,128)(2,1)} async-done(((bf16[8,768,384]{2,1,0:T(8,128)(2,1)}), bf16[8,768,768]{2,1,0:T(8,128)(2,1)}) %all-gather.10.cloned.1.call-update) | async-done | bytes 9437200 | tf_op jit(solution)/shard_map/all_gather | solution.py:49
  359.0 5.1 fusion.80
  364.1 1.7 copy-done.1
  366.1 10.2 gather_fusion.1
  376.2 8.2 gather.23
  384.5 11.2 multiply_reduce_fusion.1
  395.7 38.0 %reduce-scatter.12.cloned.1.call-done = f32[1,256,768]{2,1,0:T(8,128)} async-done(((f32[4,256,768]{2,1,0:T(8,128)}), f32[1,256,768]{2,1,0:T(8,128)}) %reduce-scatter.12.cloned.1.call-update) | async-done | bytes 786448 | tf_op jit(solution)/shard_map/reduce_scatter | solution.py:160
  434.4 13.3 %psum.37 = f32[]{:T(128)} all-reduce(f32[]{:T(128)} %convert_reduce_fusion.1), channel_id=1, replica_groups=mesh['fsdp'=2,'heads'=4,'tensor'=4] {'fsdp','tensor'}, use_global_device_ids=true, to_apply=%region_20.21 | all-reduce | flops 1 | bytes 8 | tf_op jit(solution)/shard_map/psum | solution.py:74
  448.4 31.4 %all-reduce.13.cloned.1.call-done = f32[1,256,768]{2,1,0:T(8,128)} async-done(((f32[1,256,768]{2,1,0:T(8,128)}), f32[1,256,768]{2,1,0:T(8,128)}) %all-reduce.13.cloned.1.call-update) | async-done | bytes 786448 | tf_op jit(solution)/shard_map/psum | solution.py:159
  479.8 2.4 multiply_convert_fusion.2
  482.5 18.9 %all-gather.12.cloned.1.call-done = bf16[4,256,768]{2,1,0:T(8,128)(2,1)} async-done(((bf16[1,256,768]{2,1,0:T(8,128)(2,1)}), bf16[4,256,768]{2,1,0:T(8,128)(2,1)}) %all-gather.12.cloned.1.call-update) | async-done | bytes 1572880 | tf_op jit(solution)/shard_map/all_gather | solution.py:175
  501.4 6.1 gather_fusion.2
  507.5 1.2 copy-done.10
  508.7 6.4 fusion.9
  515.1 7.3 fusion.81
  522.4 10.2 gather_fusion.3
  532.6 8.2 gather.26
  540.8 11.2 multiply_reduce_fusion
  554.6 1.8 fusion.1
  556.4 9.7 gather_fusion.4
  566.8 6.0 all-reduce.2
  572.9 17.4 %reduce-scatter.14.cloned.1.call-done = f32[1,256,768]{2,1,0:T(8,128)} async-done(((f32[4,256,768]{2,1,0:T(8,128)}), f32[1,256,768]{2,1,0:T(8,128)}) %reduce-scatter.14.cloned.1.call-update) | async-done | bytes 786448 | tf_op jit(solution)/shard_map/reduce_scatter | solution.py:209
  591.0 11.7 psum.39
  604.6 31.7 %all-reduce.15.cloned.1.call-done = f32[1,256,768]{2,1,0:T(8,128)} async-done(((f32[1,256,768]{2,1,0:T(8,128)}), f32[1,256,768]{2,1,0:T(8,128)}) %all-reduce.15.cloned.1.call-update) | async-done | bytes 786448 | tf_op jit(solution)/shard_map/psum | solution.py:212
  636.3 2.3 multiply_reduce_fusion.2
  638.6 1.6 multiply_add_fusion
  640.2 2.1 convolution_convert_fusion.1
  642.3 2.0 fusion.49
  644.3 1.6 copy.176
  645.9 1.7 reshape.523
  647.7 1.3 multiply_reduce_fusion.3
  650.3 2.1 fusion.45
  652.4 10.5 fusion.82
  663.1 1.3 copy-done.9
  664.9 7.9 fusion.16
  672.8 1.1 copy-done.27
  674.5 1.3 collective-permute-start
  675.8 18.0 %collective-permute-done = f32[1,256,768]{2,1,0:T(8,128)S(1)} collective-permute-done((f32[1,256,768]{2,1,0:T(8,128)S(1)}, f32[1,256,768]{2,1,0:T(8,128)S(1)}, u32[]{:S(2)}, u32[]{:S(2)}) %collective-permute-start) | collective-permute-done | bytes 786464 | tf_op jit(solution)/shard_map/ppermute | solution.py:277
  693.9 1.6 collective-permute-start.1
  696.9 1.5 copy.179
  699.0 11.5 reduce-scatter.22.cloned.1.call-done
  712.4 17.8 %collective-permute-done.1 = f32[1,256,768]{2,1,0:T(8,128)S(1)} collective-permute-done((f32[1,256,768]{2,1,0:T(8,128)S(1)}, f32[1,256,768]{2,1,0:T(8,128)S(1)}, u32[]{:S(2)}, u32[]{:S(2)}) %collective-permute-start.1) | collective-permute-done | bytes 786464 | tf_op jit(solution)/shard_map/ppermute | solution.py:277
  731.1 13.9 %all-reduce.5 = (f32[768]{0:T(1024)S(1)}, f32[768]{0:T(1024)S(1)}) all-reduce(f32[768]{0:T(1024)} %get-tuple-element.14, f32[768]{0:T(1024)S(1)} %copy-done.60), channel_id=5, replica_groups=mesh['fsdp'=2,'heads'=4,'tensor'=4] {'fsdp','tensor'}, use_global_device_ids=true, to_apply=%region_35.36.clone | all-reduce | flops 1536 | bytes 12288
  747.6 1.2 fusion.37
  748.8 8.3 reduce-scatter.16.cloned.1.call-done
  757.1 214.7 %reduce-scatter.18.cloned.1.call-done = f32[8,384,768]{2,1,0:T(8,128)} async-done(((f32[8,768,768]{2,1,0:T(8,128)}), f32[8,384,768]{2,1,0:T(8,128)}) %reduce-scatter.18.cloned.1.call-update) | async-done | bytes 9437200 | tf_op jit(solution)/shard_map/reduce_scatter | solution.py:56
  971.7 214.6 %reduce-scatter.20.cloned.1.call-done = f32[8,768,384]{2,1,0:T(8,128)} async-done(((f32[8,768,768]{2,1,0:T(8,128)}), f32[8,768,384]{2,1,0:T(8,128)}) %reduce-scatter.20.cloned.1.call-update) | async-done | bytes 9437200 | tf_op jit(solution)/shard_map/reduce_scatter | solution.py:57
  (244 shorter events, 30.5 us)
Async XLA Ops:
  7.2 16.8 %copy-start.63 = (u32[32]{0:T(128)S(1)}, u32[32]{0:T(128)}, u32[]{:S(2)}) copy-start(u32[32]{0:T(128)} %constant.143) | copy-start | bytes 388
  7.2 18.1 %copy-start.66 = (bf16[96]{0:T(256)(128)(2,1)S(1)}, bf16[96]{0:T(256)(128)(2,1)}, u32[]{:S(2)}) copy-start(bf16[96]{0:T(256)(128)(2,1)} %param.15) | copy-start | bytes 580
  7.2 18.4 %copy-start.67 = (bf16[96]{0:T(256)(128)(2,1)S(1)}, bf16[96]{0:T(256)(128)(2,1)}, u32[]{:S(2)}) copy-start(bf16[96]{0:T(256)(128)(2,1)} %param.18) | copy-start | bytes 580
  7.2 31.8 %copy-start.12 = (bf16[1,256,768]{2,1,0:T(8,128)(2,1)S(1)}, bf16[1,256,768]{2,1,0:T(8,128)(2,1)}, u32[]{:S(2)}) copy-start(bf16[1,256,768]{2,1,0:T(8,128)(2,1)} %param.11) | copy-start | bytes 1179652
  7.2 90.4 %all-reduce.11.cloned.1.call-start = ((), (), s32[]{:S(2)}) async-start(), calls=%async_computation.7 | async-start | bytes 1572864 | tf_op jit(solution)/shard_map/psum | solution.py:115
  23.0 17.6 %copy-start.64 = (s32[1,256]{1,0:T(1,128)S(1)}, s32[1,256]{1,0:T(1,128)}, u32[]{:S(2)}) copy-start(s32[1,256]{1,0:T(1,128)} %param.12) | copy-start | bytes 3076
  23.9 18.3 %copy-start.26 = (bf16[768,3,192]{0,2,1:T(8,128)(2,1)}, bf16[768,3,192]{0,2,1:T(8,128)(2,1)S(1)}, u32[]{:S(2)}) copy-start(bf16[768,3,192]{0,2,1:T(8,128)(2,1)S(1)} %copy.140) | copy-start | bytes 2654212
  39.0 3.2 copy-start.41
  41.9 11.5 copy-start.59
  42.2 57.0 %copy-start.33 = (bf16[256,3,64]{0,2,1:T(8,128)(2,1)}, bf16[256,3,64]{0,2,1:T(8,128)(2,1)S(1)}, u32[]{:S(2)}) copy-start(bf16[256,3,64]{0,2,1:T(8,128)(2,1)S(1)} %fusion.25) | copy-start | bytes 294916
  52.2 48.6 %copy-start.23 = (bf16[3,64,768]{2,1,0:T(8,128)(2,1)}, bf16[3,64,768]{2,1,0:T(8,128)(2,1)S(1)}, u32[]{:S(2)}) copy-start(bf16[3,64,768]{2,1,0:T(8,128)(2,1)S(1)} %copy.143) | copy-start | bytes 884740
  53.4 80.5 %all-gather.6.cloned.1.call-start = ((), (), s32[]{:S(2)}) async-start(), calls=%async_computation.8 | async-start | bytes 1966080 | tf_op jit(solution)/shard_map/all_gather | solution.py:119
  53.5 48.0 %copy-start.43 = (f32[768]{0:T(1024)}, f32[768]{0:T(1024)S(1)}, u32[]{:S(2)}) copy-start(f32[768]{0:T(1024)S(1)} %convert_element_type.117) | copy-start | bytes 9220
  98.9 2.6 copy-start.52
  100.8 138.8 %all-gather.8.cloned.1.call-start = ((), (), s32[]{:S(2)}) async-start(), calls=%async_computation.9 | async-start | bytes 14155776 | tf_op jit(solution)/shard_map/all_gather | solution.py:48
  101.5 257.5 %all-gather.10.cloned.1.call-start = ((), (), s32[]{:S(2)}) async-start(), calls=%async_computation.10 | async-start | bytes 14155776 | tf_op jit(solution)/shard_map/all_gather | solution.py:49
  102.1 11.8 copy-start.61
  102.1 331.6 %reduce-scatter.12.cloned.1.call-start = ((), (), s32[]{:S(2)}) async-start(), calls=%async_computation.11 | async-start | bytes 3932160 | tf_op jit(solution)/shard_map/reduce_scatter | solution.py:160
  125.2 8.7 copy-start.62
  133.3 7.1 copy-start.48
  133.9 6.5 copy-start
  140.4 105.3 %copy-start.17 = (bf16[1024,768]{1,0:T(8,128)(2,1)}, bf16[1024,768]{1,0:T(8,128)(2,1)S(1)}, u32[]{:S(2)}) copy-start(bf16[1024,768]{1,0:T(8,128)(2,1)S(1)} %gather_fusion) | copy-start | bytes 4718596
  151.8 355.8 %copy-start.46 = (f32[1024]{0:T(1024)}, f32[1024]{0:T(1024)S(1)}, u32[]{:S(2)}) copy-start(f32[1024]{0:T(1024)S(1)} %scatter_custom_fusion.1) | copy-start | bytes 12292
  254.4 104.6 %copy-start.8 = (bf16[8,128,768]{2,1,0:T(8,128)(2,1)}, bf16[8,128,768]{2,1,0:T(8,128)(2,1)S(1)}, u32[]{:S(2)}) copy-start(bf16[8,128,768]{2,1,0:T(8,128)(2,1)S(1)} %fusion.4) | copy-start | bytes 4718596
  376.2 8.2 copy-start.18
  395.6 38.2 %copy-start.65 = (s32[1,256]{1,0:T(1,128)S(1)}, s32[1,256]{1,0:T(1,128)}, u32[]{:S(2)}) copy-start(s32[1,256]{1,0:T(1,128)} %param.12) | copy-start | bytes 3076
  395.6 84.2 %copy-start.4 = (f32[1,256,768]{2,1,0:T(8,128)S(1)}, f32[1,256,768]{2,1,0:T(8,128)}, u32[]{:S(2)}) copy-start(f32[1,256,768]{2,1,0:T(8,128)} %copy-done.3) | copy-start | bytes 2359300
  395.6 84.2 %copy-start.34 = (bf16[1,256,768]{2,1,0:T(8,128)(2,1)S(1)}, bf16[1,256,768]{2,1,0:T(8,128)(2,1)}, u32[]{:S(2)}) copy-start(bf16[1,256,768]{2,1,0:T(8,128)(2,1)} %param.14) | copy-start | bytes 1179652
  395.7 105.8 %copy-start.49 = (s32[1024]{0:T(1024)S(1)}, s32[1024]{0:T(1024)}, u32[]{:S(2)}) copy-start(s32[1024]{0:T(1024)} %copy-done.48) | copy-start | bytes 12292
  395.7 84.1 %all-reduce.13.cloned.1.call-start = ((), (), s32[]{:S(2)}) async-start(), calls=%async_computation.12 | async-start | bytes 1572864 | tf_op jit(solution)/shard_map/psum | solution.py:159
  433.8 67.6 %all-gather.12.cloned.1.call-start = ((), (), s32[]{:S(2)}) async-start(), calls=%async_computation.13 | async-start | bytes 1966080 | tf_op jit(solution)/shard_map/all_gather | solution.py:175
  482.3 108.0 %reduce-scatter.14.cloned.1.call-start = ((), (), s32[]{:S(2)}) async-start(), calls=%async_computation.14 | async-start | bytes 3932160 | tf_op jit(solution)/shard_map/reduce_scatter | solution.py:209
  515.1 7.3 copy-start.15
  532.6 8.2 copy-start.19
  552.0 2.6 copy-start.2
  552.0 84.3 %all-reduce.15.cloned.1.call-start = ((), (), s32[]{:S(2)}) async-start(), calls=%async_computation.15 | async-start | bytes 1572864 | tf_op jit(solution)/shard_map/psum | solution.py:212
  556.4 47.0 %copy-start.30 = (f32[1024,32]{0,1:T(8,128)S(1)}, f32[1024,32]{0,1:T(8,128)}, u32[]{:S(2)}) copy-start(f32[1024,32]{0,1:T(8,128)} %copy-done.29) | copy-start | bytes 393220
  556.4 47.1 %copy-start.20 = (bf16[1,256,768]{2,1,0:T(8,128)(2,1)S(1)}, bf16[1,256,768]{2,1,0:T(8,128)(2,1)}, u32[]{:S(2)}) copy-start(bf16[1,256,768]{2,1,0:T(8,128)(2,1)} %multiply_convert_fusion.1) | copy-start | bytes 1179652
  566.1 70.2 %copy-start.5 = (f32[1,256,768]{2,1,0:T(8,128)S(1)}, f32[1,256,768]{2,1,0:T(8,128)}, u32[]{:S(2)}) copy-start(f32[1,256,768]{2,1,0:T(8,128)} %copy-done.3) | copy-start | bytes 2359300
  566.1 70.2 %copy-start.31 = (bf16[768,32]{0,1:T(8,128)(2,1)S(1)}, bf16[768,32]{0,1:T(8,128)(2,1)}, u32[]{:S(2)}) copy-start(bf16[768,32]{0,1:T(8,128)(2,1)} %reshape.512) | copy-start | bytes 147460
  566.1 70.2 %copy-start.44 = (f32[768]{0:T(1024)S(1)}, f32[768]{0:T(1024)}, u32[]{:S(2)}) copy-start(f32[768]{0:T(1024)} %copy-done.43) | copy-start | bytes 9220
  566.1 70.2 %copy-start.53 = (f32[256]{0:T(256)S(1)}, f32[256]{0:T(256)}, u32[]{:S(2)}) copy-start(f32[256]{0:T(256)} %copy-done.52) | copy-start | bytes 3076
  566.1 70.2 %copy-start.58 = (f32[256]{0:T(256)S(1)}, f32[256]{0:T(256)}, u32[]{:S(2)}) copy-start(f32[256]{0:T(256)} %copy-done.57) | copy-start | bytes 3076
  566.2 72.4 %copy-start.22 = (f32[1,256,768]{2,1,0:T(8,128)S(1)}, f32[1,256,768]{2,1,0:T(8,128)}, u32[]{:S(2)}) copy-start(f32[1,256,768]{2,1,0:T(8,128)} %get-tuple-element.24) | copy-start | bytes 2359300
  590.3 106.6 %reduce-scatter.24.cloned.1.call-start = ((), (), s32[]{:S(2)}) async-start(), calls=%async_computation.20 | async-start | bytes 442368
  604.6 106.0 %reduce-scatter.22.cloned.1.call-start = ((), (), s32[]{:S(2)}) async-start(), calls=%async_computation.19 | async-start | bytes 884736
  640.2 7.4 copy-start.13
  642.3 5.4 copy-start.7
  647.6 2.3 copy-start.28
  647.6 2.6 copy-start.42
  647.6 2.6 copy-start.51
  647.7 2.6 copy-start.55
  649.2 107.9 %reduce-scatter.16.cloned.1.call-start = ((), (), s32[]{:S(2)}) async-start(), calls=%async_computation.16 | async-start | bytes 2654208 | tf_op jit(solution)/shard_map/reduce_scatter | solution.py:285
  649.7 2.6 copy-start.35
  649.9 2.4 copy-start.37
  649.9 2.5 copy-start.16
  650.3 12.7 %copy-start.39 = (bf16[256,3,64]{0,2,1:T(8,128)(2,1)}, bf16[256,3,64]{0,2,1:T(8,128)(2,1)S(1)}, u32[]{:S(2)}) copy-start(bf16[256,3,64]{0,2,1:T(8,128)(2,1)S(1)} %fusion.26) | copy-start | bytes 294916
  652.4 319.4 %reduce-scatter.18.cloned.1.call-start = ((), (), s32[]{:S(2)}) async-start(), calls=%async_computation.17 | async-start | bytes 28311552 | tf_op jit(solution)/shard_map/reduce_scatter | solution.py:56
  663.0 523.3 %reduce-scatter.20.cloned.1.call-start = ((), (), s32[]{:S(2)}) async-start(), calls=%async_computation.18 | async-start | bytes 28311552 | tf_op jit(solution)/shard_map/reduce_scatter | solution.py:57
  674.0 56.1 %copy-start.56 = (f32[256]{0:T(256)S(1)}, f32[256]{0:T(256)}, u32[]{:S(2)}) copy-start(f32[256]{0:T(256)} %copy-done.54) | copy-start | bytes 3076
  674.5 56.6 %copy-start.60 = (f32[768]{0:T(1024)S(1)}, f32[768]{0:T(1024)}, u32[]{:S(2)}) copy-start(f32[768]{0:T(1024)} %get-tuple-element.12) | copy-start | bytes 9220
  674.5 73.1 %copy-start.14 = (f32[1,256,768]{2,1,0:T(8,128)S(1)}, f32[1,256,768]{2,1,0:T(8,128)}, u32[]{:S(2)}) copy-start(f32[1,256,768]{2,1,0:T(8,128)} %copy-done.13) | copy-start | bytes 2359300
  674.5 19.3 %collective-permute-start = (f32[1,256,768]{2,1,0:T(8,128)S(1)}, f32[1,256,768]{2,1,0:T(8,128)S(1)}, u32[]{:S(2)}, u32[]{:S(2)}) collective-permute-start(f32[1,256,768]{2,1,0:T(8,128)S(1)} %convolution_bitcast_fusion), channel_id=1, source_target_pairs={{0,4},{4,0},{8,12},{12,8},{1,5},{5,1},{9,13},{13,9},{2,6},{6,2},{1... | collective-permute-start | bytes 2359304 | tf_op jit(solution)/shard_map/ppermute | solution.py:277
  693.9 36.2 %collective-permute-start.1 = (f32[1,256,768]{2,1,0:T(8,128)S(1)}, f32[1,256,768]{2,1,0:T(8,128)S(1)}, u32[]{:S(2)}, u32[]{:S(2)}) collective-permute-start(f32[1,256,768]{2,1,0:T(8,128)S(1)} %add.145), channel_id=1, source_target_pairs={{0,8},{4,12},{8,0},{12,4},{1,9},{5,13},{9,1},{13,5},{2,10},{6,14},... | collective-permute-start | bytes 2359304 | tf_op jit(solution)/shard_map/ppermute | solution.py:277
  (21 other events, 25.3 us)
Sparse Core Ops, SparseCore 0:
  53.5 44.0 all-reduce.10
  100.9 18.9 all-gather.5
  121.5 118.0 all-gather.7
  241.0 117.9 all-gather.9
  395.8 37.9 reduce-scatter.11
  436.1 43.6 all-reduce.12
  482.4 18.9 all-gather.11
  552.1 38.0 reduce-scatter.13
  592.6 43.6 all-reduce.14
  639.2 33.1 reduce-scatter.23
  675.6 34.9 reduce-scatter.21
  714.4 42.6 reduce-scatter.15
  760.1 211.6 reduce-scatter.17
  974.6 211.6 reduce-scatter.19
